TPU v7x, 512 devices: a whole 4x4x16 slice. The times are simulated.
512 devices in a mesh: slab: 16 (over z_lo, y), rcv: 32 (over x, z_hi, core).
Axes of the slice: x: 4, y: 4, z: 16 (z_hi: 4, z_lo: 4; z = z_hi * 4 + z_lo), core: 2. Of those that a mesh axis runs over, the one named last changes fastest.
Arguments:
- adjoint_now: float32 [32, 64, 128, 128], P('rcv', 'slab'), may hold values from -6 to 6
- adjoint_before: float32 [32, 64, 128, 128], P('rcv', 'slab'), may hold values from -6 to 6
- courant_field: float32 [64, 128, 128], P('slab'), may hold values from 0.04 to 0.2
- log_buoyancy: float32 [64, 128, 128], P('slab'), may hold values from -0.3 to 0.3
- snapshot_store: float32 [32, 64, 128, 128], P('rcv', 'slab'), may hold values from -6 to 6
- owner_order: int32 [32], replicated, may hold values from 0 to 31, each once
- receiver_cells: int32 [32], P('rcv'), may hold values from 0 to 1048575
- receiver_traces: float32 [32, 8], P('rcv'), may hold values from -6 to 6
- residual_weights: float32 [32], P('rcv'), may hold values from -0.3 to 0.3
Outputs:
- sensitivity: float32 [64, 128, 128], P('slab', 'rcv')
- adjoint_after: float32 [32, 64, 128, 128], P('rcv', 'slab')
Inputs may be any that keep to these rules, and one draw needn't show every extreme that they name: Each slot number appears once; checkpoint k reads slot owner_order[k] for k < 4. `receiver_cells`: a cell of the grid.
All inputs are finite; a program needn't handle non-finite values.
Results may differ from a plain program's by a relative error of at most 0.0003.
Values sent between devices are 32-bit elements; how exact they have to be, the bound alone decides.
A program may use at most 64 MiB of HBM per device.

v0:
```python
import jax
import jax.numpy as jnp
from jax import lax
from jax.sharding import PartitionSpec as P

SNAPS = 4


def extended(shard, sides, width):
    for axis, dim in sides:
        peers, length = (lax.axis_size(axis), shard.shape[dim])
        up = [(i, (i + 1) % peers) for i in range(peers - 1)]
        down = [(j, i) for i, j in up]
        last = lax.slice_in_dim(shard, length - width, length, axis=dim)
        leading = lax.slice_in_dim(shard, 0, width, axis=dim)
        before = lax.ppermute(last, axis, up)
        after = lax.ppermute(leading, axis, down)
        shard = jnp.concatenate([before, shard, after], axis=dim)
    return shard


def from_root(block, axis, owner):
    block = jnp.where(lax.axis_index(axis) == owner, block, jnp.zeros_like(block))
    return lax.psum(block, axis)


def piece_of(field, axis_no, begin, extent):
    return lax.slice_in_dim(field, begin, begin + extent, axis=axis_no)


def pad_axis(field, axis_no):
    widths = [(0, 0)] * field.ndim
    widths[axis_no] = (2, 2)
    return jnp.pad(field, widths)


def second_diff(field, axis_no, extent):
    outer = piece_of(field, axis_no, 0, extent) + piece_of(field, axis_no, 4, extent)
    inner = piece_of(field, axis_no, 1, extent) + piece_of(field, axis_no, 3, extent)
    return (16.0 * inner - outer - 30.0 * piece_of(field, axis_no, 2, extent)) / 12.0


def first_diff(field, axis_no, extent):
    inner = piece_of(field, axis_no, 3, extent) - piece_of(field, axis_no, 1, extent)
    outer = piece_of(field, axis_no, 4, extent) - piece_of(field, axis_no, 0, extent)
    return (8.0 * inner - outer) / 12.0


def slopes(log_ext):
    width = log_ext.shape[0] - 4
    centre = piece_of(log_ext, 0, 2, width)
    wide_y = pad_axis(centre, 1)
    wide_z = pad_axis(centre, 2)
    return jnp.stack(
        [
            first_diff(log_ext, 0, width),
            first_diff(wide_y, 1, centre.shape[1]),
            first_diff(wide_z, 2, centre.shape[2]),
        ]
    )


def advance(field, before, courant, gradient):
    first_axis = field.ndim - 3
    width = field.shape[first_axis] - 4
    centre = piece_of(field, first_axis, 2, width)
    wide_y = pad_axis(centre, first_axis + 1)
    wide_z = pad_axis(centre, first_axis + 2)
    size_y = field.shape[first_axis + 1]
    size_z = field.shape[first_axis + 2]
    curvature = (
        second_diff(field, first_axis, width)
        + second_diff(wide_y, first_axis + 1, size_y)
        + second_diff(wide_z, first_axis + 2, size_z)
    )
    drift_term = (
        gradient[0] * first_diff(field, first_axis, width)
        + gradient[1] * first_diff(wide_y, first_axis + 1, size_y)
        + gradient[2] * first_diff(wide_z, first_axis + 2, size_z)
    )
    return 2.0 * centre - before + courant * (curvature + drift_term)


def local(
    adjoint_now,
    adjoint_before,
    courant_field,
    log_buoyancy,
    snapshot_store,
    owner_order,
    receiver_cells,
    receiver_traces,
    residual_weights,
):
    slab_rows = courant_field.shape[0]
    size_y = courant_field.shape[1]
    size_z = courant_field.shape[2]
    grid_rows = slab_rows * lax.axis_size("slab")
    row_anchor = lax.axis_index("slab") * slab_rows
    model_ext = extended(jnp.stack([courant_field, log_buoyancy]), (("slab", 1),), 4)
    courant_ext = model_ext[0, 2 : slab_rows + 6]
    gradient = slopes(model_ext[1])
    plane_ids = lax.broadcasted_iota(
        jnp.int32, (size_y, size_z), 0
    ) * size_z + lax.broadcasted_iota(jnp.int32, (size_y, size_z), 1)
    cell_column = receiver_cells[:, None, None, None]

    def evolve(field, before, offset, width, tick):
        upcoming = advance(
            field,
            before,
            courant_ext[offset - 2 : offset - 2 + width],
            gradient[:, offset - 2 : offset - 2 + width],
        )
        global_rows = row_anchor - 4 + offset + lax.broadcasted_iota(jnp.int32, (width,), 0)
        flat_ids = global_rows[:, None, None] * (size_y * size_z) + plane_ids[None]
        amplitude = receiver_traces[:, tick][:, None, None, None]
        upcoming = upcoming + jnp.where(flat_ids[None] == cell_column, amplitude, 0.0)
        return (upcoming, global_rows)

    current = adjoint_now
    previous = adjoint_before
    kernel_sum = jnp.zeros((slab_rows, size_y, size_z), jnp.float32)
    for snap_index in range(SNAPS):
        forward_field = from_root(snapshot_store[0], "rcv", owner_order[snap_index])
        current_ext = extended(current, (("slab", 1),), 4)
        previous_ext = extended(previous, (("slab", 1),), 2)
        middle, middle_rows = evolve(current_ext, previous_ext, 2, slab_rows + 4, 2 * snap_index)
        inside = (middle_rows >= 0) & (middle_rows < grid_rows)
        middle = jnp.where(inside[None, :, None, None], middle, 0.0)
        latest, unused_rows = evolve(middle, current, 4, slab_rows, 2 * snap_index + 1)
        previous = middle[:, 2 : slab_rows + 2]
        current = latest
        kernel_terms = jnp.sum(
            residual_weights[:, None, None, None] * current * forward_field, axis=0
        )
        kernel_sum = kernel_sum + kernel_terms
    sensitivity = lax.psum_scatter(kernel_sum, "rcv", scatter_dimension=1, tiled=True)
    return (sensitivity, current)


def solution(mesh):
    placed = (
        P("rcv", "slab", None, None),
        P("rcv", "slab", None, None),
        P("slab", None, None),
        P("slab", None, None),
        P("rcv", "slab", None, None),
        P(),
        P("rcv"),
        P("rcv", None),
        P("rcv"),
    )
    return jax.shard_map(
        local,
        mesh=mesh,
        in_specs=placed,
        out_specs=(P("slab", "rcv", None), P("rcv", "slab", None, None)),
        check_vma=False,
    )
```

profile of v0, /device:TPU:1, one launch (start us, length us, event | category | flops | bytes accessed | tf_op | source)
XLA Modules:
  0.0 783.1 jit_solution(6446867127906794386)
XLA Ops:
  7.2 0.0 copy-start.13
  7.2 0.0 all-reduce.25.cloned.1.call-start
  7.2 1.1 pad_maximum_fusion.8
  8.3 4.1 collective-permute-start.4
  12.4 1.3 collective-permute-start.5
  13.7 4.0 collective-permute-start
  17.7 1.3 collective-permute-start.1
  19.0 1.7 fusion.45
  20.7 4.6 collective-permute-start.2
  25.3 0.1 iota_add_fusion
  25.4 0.7 fusion.46
  26.8 1.3 collective-permute-start.3
  28.1 0.0 copy-start
  28.1 0.0 copy-start.9
  28.2 0.1 constant_dynamic-update-slice_fusion.1
  28.2 0.9 collective-permute-done.1
  29.2 0.0 copy-start.12
  29.3 0.1 pad_maximum_fusion
  29.5 0.6 copy-done.10
  30.1 0.2 copy-done.11
  30.3 4.7 collective-permute-done.3
  34.9 3.5 fusion.12
  38.4 0.0 copy-start.7
  38.5 0.0 copy-start.17
  38.5 2.0 fusion.37
  40.5 4.1 collective-permute-start.6
  44.6 1.3 collective-permute-start.7
  45.9 0.7 fusion.47
  49.2 0.0 copy-start.8
  49.2 1.0 fusion.44
  50.2 4.0 collective-permute-start.8
  54.2 1.3 collective-permute-start.9
  55.5 1.2 pad_maximum_fusion.1
  56.7 5.1 collective-permute-done.9
  61.8 2.9 fusion.15
  64.8 0.0 copy-start.15
  64.8 2.9 fusion.34
  67.6 4.3 collective-permute-start.10
  72.0 1.3 collective-permute-start.11
  73.3 1.0 broadcast_select_fusion.3
  74.3 0.0 all-reduce.25.cloned.1.call-update
  74.3 0.0 all-reduce.23.cloned.1.call-start
  74.4 1.0 fusion.43
  75.4 4.1 collective-permute-start.12
  79.5 1.3 collective-permute-start.13
  80.8 1.2 pad_maximum_fusion.2
  82.0 5.3 collective-permute-done.13
  87.3 3.0 fusion.18
  90.4 2.2 fusion.31
  92.5 4.2 collective-permute-start.14
  96.7 1.3 collective-permute-start.15
  98.7 4.6 collective-permute-start.16
  103.3 1.3 collective-permute-start.17
  104.6 0.1 pad_maximum_fusion.3
  104.7 1.8 collective-permute-done.16
  106.5 5.7 collective-permute-done.17
  112.2 1.8 fusion.21
  114.0 0.8 copy-done.3
  114.8 318.7 %all-reduce.25.cloned.1.call-done = (f32[1,4,128,128]{3,2,1,0:T(8,128)}, f32[1,4,128,128]{3,2,1,0:T(8,128)}, f32[1,4,128,128]{3,2,1,0:T(8,128)}, f32[1,4,128,128]{3,2,1,0:T(8,128)}) async-done(((f32[1,4,128,128]{3,2,1,0:T(8,128)}, f32[1,4,128,128]{3,2,1,0:T(8,128)}, f32[1,4,128,128]{3,2,1,0:T(8,128)}, f32[1,4,128,128]{3,2,1,0:T(8,128)}), (f32[1,4,128,128]{3,2,1,0:T(8,128)}, f32[1,4,128,128]{3,2,1,0:T(8,128)}, ...) | async-done | bytes 1048592 | tf_op jit(solution)/shard_map/psum | solution.py:24
  433.5 3.8 add_bitcast_fusion
  437.3 0.0 all-reduce.23.cloned.1.call-update
  437.3 1.3 dynamic-slice
  439.2 335.7 %all-reduce.23.cloned.1.call-done = f32[4,128,128]{2,1,0:T(8,128)} async-done(((f32[4,128,128]{2,1,0:T(8,128)}), f32[4,128,128]{2,1,0:T(8,128)}) %all-reduce.23.cloned.1.call-update) | async-done | bytes 262160
  774.9 1.3 constant_dynamic-slice_fusion
  (53 shorter events, 0.5 us)
Async XLA Ops:
  7.2 21.0 %copy-start.13 = (f32[1,4,128,128]{3,2,1,0:T(8,128)S(1)}, f32[1,4,128,128]{3,2,1,0:T(8,128)}, u32[]{:S(2)}) copy-start(f32[1,4,128,128]{3,2,1,0:T(8,128)} %param.9) | copy-start | bytes 786436
  7.2 18.2 %copy-start.16 = (f32[1,8]{1,0:T(1,128)S(1)}, f32[1,8]{1,0:T(1,128)}, u32[]{:S(2)}) copy-start(f32[1,8]{1,0:T(1,128)} %param.16) | copy-start | bytes 100
  7.2 426.3 %all-reduce.25.cloned.1.call-start = ((), (), s32[]{:S(2)}) async-start(), calls=%async_computation.1 | async-start | bytes 2097152 | tf_op jit(solution)/shard_map/psum | solution.py:24
  8.3 21.0 %collective-permute-start.4 = (f32[2,4,128,128]{3,2,1,0:T(8,128)S(1)}, f32[2,4,128,128]{3,2,1,0:T(8,128)S(1)}, u32[]{:S(2)}, u32[]{:S(2)}) collective-permute-start(f32[2,4,128,128]{3,2,1,0:T(8,128)S(1)} %pad_maximum_fusion.8), channel_id=1, source_target_pairs={{0,32},{32,64},{64,96},{96,128},{128,160},{160,192},{192,224},{224... | collective-permute-start | bytes 1572872 | tf_op jit(solution)/shard_map/ppermute | solution.py:16
  12.4 16.9 %collective-permute-start.5 = (f32[2,4,128,128]{3,2,1,0:T(8,128)S(1)}, f32[2,4,128,128]{3,2,1,0:T(8,128)S(1)}, u32[]{:S(2)}, u32[]{:S(2)}) collective-permute-start(f32[2,4,128,128]{3,2,1,0:T(8,128)S(1)} %pad_maximum_fusion.8), channel_id=1, source_target_pairs={{32,0},{64,32},{96,64},{128,96},{160,128},{192,160},{224,192},{256... | collective-permute-start | bytes 1572872 | tf_op jit(solution)/shard_map/ppermute | solution.py:17
  13.7 13.1 %collective-permute-start = (f32[1,4,128,128]{3,2,1,0:T(8,128)}, f32[1,4,128,128]{3,2,1,0:T(8,128)S(1)}, u32[]{:S(2)}, u32[]{:S(2)}) collective-permute-start(f32[1,4,128,128]{3,2,1,0:T(8,128)} %param.9), channel_id=1, source_target_pairs={{0,32},{32,64},{64,96},{96,128},{128,160},{160,192},{192,224},{224... | collective-permute-start | bytes 786440 | tf_op jit(solution)/shard_map/ppermute | solution.py:16
  17.7 11.5 %collective-permute-start.1 = (f32[1,4,128,128]{3,2,1,0:T(8,128)}, f32[1,4,128,128]{3,2,1,0:T(8,128)S(1)}, u32[]{:S(2)}, u32[]{:S(2)}) collective-permute-start(f32[1,4,128,128]{3,2,1,0:T(8,128)} %param.9), channel_id=1, source_target_pairs={{32,0},{64,32},{96,64},{128,96},{160,128},{192,160},{224,192},{256... | collective-permute-start | bytes 786440 | tf_op jit(solution)/shard_map/ppermute | solution.py:17
  20.7 9.6 %collective-permute-start.2 = (f32[1,2,128,128]{3,2,1,0:T(8,128)}, f32[1,2,128,128]{3,2,1,0:T(8,128)}, u32[]{:S(2)}, u32[]{:S(2)}) collective-permute-start(f32[1,2,128,128]{3,2,1,0:T(8,128)} %get-tuple-element.25), channel_id=1, source_target_pairs={{0,32},{32,64},{64,96},{96,128},{128,160},{160,192},{192,224},{224... | collective-permute-start | bytes 393224 | tf_op jit(solution)/shard_map/ppermute | solution.py:16
  26.8 8.2 %collective-permute-start.3 = (f32[1,2,128,128]{3,2,1,0:T(8,128)}, f32[1,2,128,128]{3,2,1,0:T(8,128)S(1)}, u32[]{:S(2)}, u32[]{:S(2)}) collective-permute-start(f32[1,2,128,128]{3,2,1,0:T(8,128)} %get-tuple-element.26), channel_id=1, source_target_pairs={{32,0},{64,32},{96,64},{128,96},{160,128},{192,160},{224,192},{256... | collective-permute-start | bytes 393224 | tf_op jit(solution)/shard_map/ppermute | solution.py:17
  28.1 1.2 copy-start
  28.1 1.2 copy-start.9
  29.2 5.7 copy-start.12
  29.3 0.8 copy-start.10
  29.3 1.0 copy-start.11
  34.9 3.5 copy-start.14
  38.4 2.1 copy-start.1
  38.4 6.2 copy-start.7
  38.5 7.4 copy-start.17
  40.5 15.0 %collective-permute-start.6 = (f32[1,4,128,128]{3,2,1,0:T(8,128)}, f32[1,4,128,128]{3,2,1,0:T(8,128)}, u32[]{:S(2)}, u32[]{:S(2)}) collective-permute-start(f32[1,4,128,128]{3,2,1,0:T(8,128)} %fusion.37), channel_id=1, source_target_pairs={{0,32},{32,64},{64,96},{96,128},{128,160},{160,192},{192,224},{224... | collective-permute-start | bytes 786440 | tf_op jit(solution)/shard_map/ppermute | solution.py:16
  44.6 10.9 %collective-permute-start.7 = (f32[1,4,128,128]{3,2,1,0:T(8,128)}, f32[1,4,128,128]{3,2,1,0:T(8,128)}, u32[]{:S(2)}, u32[]{:S(2)}) collective-permute-start(f32[1,4,128,128]{3,2,1,0:T(8,128)} %fusion.37), channel_id=1, source_target_pairs={{32,0},{64,32},{96,64},{128,96},{160,128},{192,160},{224,192},{256... | collective-permute-start | bytes 786440 | tf_op jit(solution)/shard_map/ppermute | solution.py:17
  49.2 12.7 %copy-start.8 = (f32[1,4,128,128]{3,2,1,0:T(8,128)S(1)}, f32[1,4,128,128]{3,2,1,0:T(8,128)}, u32[]{:S(2)}) copy-start(f32[1,4,128,128]{3,2,1,0:T(8,128)} %copy-done.7) | copy-start | bytes 786436
  50.2 6.5 collective-permute-start.8
  54.2 7.6 collective-permute-start.9
  64.7 2.9 copy-start.2
  64.8 9.5 %copy-start.5 = (f32[1,4,128,128]{3,2,1,0:T(8,128)}, f32[1,4,128,128]{3,2,1,0:T(8,128)S(1)}, u32[]{:S(2)}) copy-start(f32[1,4,128,128]{3,2,1,0:T(8,128)S(1)} %slice.739) | copy-start | bytes 786436
  64.8 8.5 %copy-start.15 = (f32[1,4,128,128]{3,2,1,0:T(8,128)S(1)}, f32[1,4,128,128]{3,2,1,0:T(8,128)}, u32[]{:S(2)}) copy-start(f32[1,4,128,128]{3,2,1,0:T(8,128)} %param.13) | copy-start | bytes 786436
  67.6 13.1 %collective-permute-start.10 = (f32[1,4,128,128]{3,2,1,0:T(8,128)}, f32[1,4,128,128]{3,2,1,0:T(8,128)}, u32[]{:S(2)}, u32[]{:S(2)}) collective-permute-start(f32[1,4,128,128]{3,2,1,0:T(8,128)} %fusion.34), channel_id=1, source_target_pairs={{0,32},{32,64},{64,96},{96,128},{128,160},{160,192},{192,224},{224... | collective-permute-start | bytes 786440 | tf_op jit(solution)/shard_map/ppermute | solution.py:16
  72.0 8.8 %collective-permute-start.11 = (f32[1,4,128,128]{3,2,1,0:T(8,128)}, f32[1,4,128,128]{3,2,1,0:T(8,128)}, u32[]{:S(2)}, u32[]{:S(2)}) collective-permute-start(f32[1,4,128,128]{3,2,1,0:T(8,128)} %fusion.34), channel_id=1, source_target_pairs={{32,0},{64,32},{96,64},{128,96},{160,128},{192,160},{224,192},{256... | collective-permute-start | bytes 786440 | tf_op jit(solution)/shard_map/ppermute | solution.py:17
  74.3 700.6 %all-reduce.23.cloned.1.call-start = ((), (), s32[]{:S(2)}) async-start(), calls=%async_computation | async-start | bytes 524288
  74.4 12.9 %copy-start.6 = (f32[1,4,128,128]{3,2,1,0:T(8,128)S(1)}, f32[1,4,128,128]{3,2,1,0:T(8,128)}, u32[]{:S(2)}) copy-start(f32[1,4,128,128]{3,2,1,0:T(8,128)} %copy-done.5) | copy-start | bytes 786436
  75.4 6.6 collective-permute-start.12
  79.5 7.8 collective-permute-start.13
  92.5 19.6 %copy-start.4 = (f32[1,4,128,128]{3,2,1,0:T(8,128)}, f32[1,4,128,128]{3,2,1,0:T(8,128)S(1)}, u32[]{:S(2)}) copy-start(f32[1,4,128,128]{3,2,1,0:T(8,128)S(1)} %fusion.31) | copy-start | bytes 786436
  92.5 12.0 %collective-permute-start.14 = (f32[1,4,128,128]{3,2,1,0:T(8,128)S(1)}, f32[1,4,128,128]{3,2,1,0:T(8,128)S(1)}, u32[]{:S(2)}, u32[]{:S(2)}) collective-permute-start(f32[1,4,128,128]{3,2,1,0:T(8,128)S(1)} %fusion.31), channel_id=1, source_target_pairs={{0,32},{32,64},{64,96},{96,128},{128,160},{160,192},{192,224},{224... | collective-permute-start | bytes 786440 | tf_op jit(solution)/shard_map/ppermute | solution.py:16
  96.7 7.9 %collective-permute-start.15 = (f32[1,4,128,128]{3,2,1,0:T(8,128)S(1)}, f32[1,4,128,128]{3,2,1,0:T(8,128)S(1)}, u32[]{:S(2)}, u32[]{:S(2)}) collective-permute-start(f32[1,4,128,128]{3,2,1,0:T(8,128)S(1)} %fusion.31), channel_id=1, source_target_pairs={{32,0},{64,32},{96,64},{128,96},{160,128},{192,160},{224,192},{256... | collective-permute-start | bytes 786440 | tf_op jit(solution)/shard_map/ppermute | solution.py:17
  98.7 7.8 collective-permute-start.16
  103.3 8.9 %collective-permute-start.17 = (f32[1,2,128,128]{3,2,1,0:T(8,128)S(1)}, f32[1,2,128,128]{3,2,1,0:T(8,128)S(1)}, u32[]{:S(2)}, u32[]{:S(2)}) collective-permute-start(f32[1,2,128,128]{3,2,1,0:T(8,128)S(1)} %get-tuple-element.13), channel_id=1, source_target_pairs={{32,0},{64,32},{96,64},{128,96},{160,128},{192,160},{224,192},{256... | collective-permute-start | bytes 393224 | tf_op jit(solution)/shard_map/ppermute | solution.py:17
  114.0 0.8 copy-start.3
Sparse Core Ops, SparseCore 0:
  74.4 359.0 all-reduce.24
  437.4 337.4 all-reduce.22
where the time goes:
time: 784 us; the launch traced here: 783 us
  waiting for transfers between devices  678 us (86%)
  starting transfers between devices  49.7 us (6%)
  other arithmetic  26.7 us (3%)
  between operations  19.1 us (2%)
  local copies, waits for them, and re-layouts  9.72 us (1%)
    unnamed x3, waiting for transfers between devices  336 us
    psum x1, waiting for transfers between devices, from_root(): return lax.psum(block, axis)  319 us
    ppermute x9, starting transfers between devices, extended(): before = lax.ppermute(last, axis, up)  38 us
    ppermute x9, waiting for transfers between devices, extended(): after = lax.ppermute(leading, axis, down)  21.6 us
  transfers between devices with their start and end apart: 20, of which 8 were waited for; matrix products, arithmetic and copies ran while one was open for 2% of the time, Pallas kernels for 0%

commit v1 on v0

v1 whole, which is shorter than its diff:
```python
import functools

import jax
import jax.numpy as jnp
from jax import lax
from jax.experimental import pallas as pl
from jax.experimental.pallas import tpu as pltpu
from jax.sharding import PartitionSpec as P

MESH = pl.DeviceIdType.MESH
F32 = jnp.float32
SNAPS = 4
STEPS = 8
CORES = 2
ZHI = 4
ROWS = 4
CHUNKS = 4
PAD = 8
A, B, M = 0, 1, 2


def when(condition, action):
    pl.when(condition)(action)


def kernel(
    dims,
    now_ref,
    before_ref,
    courant_ref,
    log_ref,
    store_ref,
    owner_ref,
    cell_ref,
    trace_ref,
    weight_ref,
    sens_ref,
    after_ref,
    field,
    log_buf,
    courant,
    grad,
    weighted,
    group_in,
    tile_out,
    tile_in,
    snap_in,
    snap_out,
    snap_tile,
    load_sem,
    model_send,
    model_recv,
    halo_send,
    halo_recv,
    group_send,
    group_recv,
    tile_send,
    tile_recv,
    snap_send,
    snap_recv,
    stile_send,
    stile_recv,
    out_sem,
):
    slabs, xs, ny, nz = dims
    group = xs * CORES
    block = ny // group
    pairs = ZHI // CORES
    chunk = ny // CHUNKS
    s = lax.axis_index("slab")
    r = lax.axis_index("rcv")
    core = lax.rem(r, CORES)
    zh = lax.rem(r // CORES, ZHI)
    xpos = r // (CORES * ZHI)
    member = xpos * CORES + core
    has_left, has_right = s > 0, s < slabs - 1

    def rcv_of(x, z, c):
        return (x * ZHI + z) * CORES + c

    def peer(d):
        other = lax.rem(member + d, group)
        return rcv_of(other // CORES, zh, lax.rem(other, CORES))

    barrier = pltpu.get_barrier_semaphore()

    def greet(slab, rcv):
        pl.semaphore_signal(barrier, 1, device_id=(slab, rcv), device_id_type=MESH)

    when(has_left, lambda: greet(s - 1, r))
    when(has_right, lambda: greet(s + 1, r))
    for d in range(1, group):
        greet(s, peer(d))
    half = zh // pairs
    for z in range(ZHI):
        when((z != zh) | (half != core), lambda: greet(s, rcv_of(xpos, z, half)))

    own = pl.ds(ROWS, ROWS)
    ycells = pl.ds(PAD, ny)
    loads = [
        pltpu.make_async_copy(log_ref, log_buf.at[own, ycells], load_sem.at[0]),
        pltpu.make_async_copy(courant_ref, courant.at[own], load_sem.at[1]),
        pltpu.make_async_copy(now_ref.at[0], field.at[A, own, ycells], load_sem.at[2]),
        pltpu.make_async_copy(before_ref.at[0], field.at[M, own, ycells], load_sem.at[3]),
        pltpu.make_async_copy(
            store_ref.at[0, :, pl.ds(pl.multiple_of(member * block, 8), block)],
            snap_in.at[group - 1],
            load_sem.at[4],
        ),
    ]
    for load in loads:
        load.start()

    zero_pad = jnp.zeros((3 * ROWS, PAD, nz), F32)
    for slot in (A, B, M):
        field[slot, :, 0:PAD, :] = zero_pad
        field[slot, :, PAD + ny : 2 * PAD + ny, :] = zero_pad
    log_buf[:, 0:PAD, :] = zero_pad
    log_buf[:, PAD + ny : 2 * PAD + ny, :] = zero_pad

    def clear(lo):
        def body(i, carry):
            rows = pl.ds(pl.multiple_of(i * 8, 8), 8)
            shifted = pl.ds(pl.multiple_of(i * 8 + PAD, 8), 8)
            zeros = jnp.zeros((8, nz), F32)
            for row in range(lo, lo + ROWS):
                for slot in (A, B, M):
                    field[slot, row, shifted, :] = zeros
                log_buf[row, shifted, :] = zeros
                courant[row, rows, :] = zeros
            return carry

        lax.fori_loop(0, ny // 8, body, 0)

    when(jnp.logical_not(has_left), lambda: clear(0))
    when(jnp.logical_not(has_right), lambda: clear(2 * ROWS))

    mine = (zh // pairs == core).astype(jnp.int32)
    neighbours = has_left.astype(jnp.int32) + has_right.astype(jnp.int32)
    pl.semaphore_wait(barrier, neighbours + (group - 1) + ZHI - mine)

    def side_copy(side, src, dst, send, recv):
        return pltpu.make_async_remote_copy(
            src_ref=src,
            dst_ref=dst,
            send_sem=send,
            recv_sem=recv,
            device_id=(s + 1 if side == 0 else s - 1, r),
            device_id_type=MESH,
        )

    leaves = (has_right, has_left)
    comes = (has_left, has_right)

    def model_copy(which, side):
        near = (2, 0)[side]
        far = (0, 2)[side]
        land_near = (2, 8)[side]
        land_far = (0, 10)[side]
        if which == 2:
            src, dst = courant_ref.at[near : near + 2], courant.at[land_near : land_near + 2]
        else:
            at, to = ((near, land_near), (far, land_far))[which]
            src, dst = log_ref.at[at : at + 2], log_buf.at[to : to + 2, ycells]
        return side_copy(side, src, dst, model_send.at[which, side], model_recv.at[which, side])

    def halo_copy(e, side, j, deep, slot, from_input=False):
        if deep == ROWS:
            at, to = 0, (0, 2 * ROWS)[side]
        else:
            at, to = (ROWS - deep, 0)[side], (ROWS - deep, 2 * ROWS)[side]
        here = pl.ds(pl.multiple_of(j * chunk, 8), chunk)
        there = pl.ds(pl.multiple_of(j * chunk + PAD, 8), chunk)
        if from_input:
            src = now_ref.at[0, at : at + deep, here]
        else:
            src = field.at[slot, ROWS + at : ROWS + at + deep, there]
        dst = field.at[slot, to : to + deep, there]
        return side_copy(side, src, dst, halo_send.at[e, side, j], halo_recv.at[e, side, j])

    def halo_start(e, j, deep, slot, from_input=False):
        for side in (0, 1):
            copy = halo_copy(e, side, j, deep, slot, from_input)
            when(leaves[side], copy.start)

    def halo_arrive(e, j, deep, slot):
        for side in (0, 1):
            copy = halo_copy(e, side, j, deep, slot)
            when(comes[side], copy.wait_recv)

    def halo_sent(e, deep, slot, from_input=False):
        def body(j, carry):
            for side in (0, 1):
                copy = halo_copy(e, side, j, deep, slot, from_input)
                when(leaves[side], copy.wait_send)
            return carry

        lax.fori_loop(0, CHUNKS, body, 0)

    for side in (0, 1):
        when(leaves[side], model_copy(0, side).start)
    for j in range(CHUNKS):
        halo_start(0, j, 2, A, True)
    for which in (1, 2):
        for side in (0, 1):
            when(leaves[side], model_copy(which, side).start)

    def snap_copy(d):
        other = lax.rem(member + d, group)
        return pltpu.make_async_remote_copy(
            src_ref=store_ref.at[0, :, pl.ds(pl.multiple_of(other * block, 8), block)],
            dst_ref=snap_in.at[d - 1],
            send_sem=snap_send.at[d - 1],
            recv_sem=snap_recv.at[d - 1],
            device_id=(s, peer(d)),
            device_id_type=MESH,
        )

    for d in range(1, group):
        snap_copy(d).start()

    lane = lax.broadcasted_iota(jnp.int32, (8, nz), 1)
    ids = lax.broadcasted_iota(jnp.int32, (8, nz), 0) * nz + lane
    low1, low2 = lane >= 1, lane >= 2
    high1, high2 = lane < nz - 1, lane < nz - 2

    def z_shifts(u):
        zero = jnp.zeros_like(u)
        return (
            jnp.where(low2, pltpu.roll(u, 2, 1), zero),
            jnp.where(low1, pltpu.roll(u, 1, 1), zero),
            jnp.where(high1, pltpu.roll(u, nz - 1, 1), zero),
            jnp.where(high2, pltpu.roll(u, nz - 2, 1), zero),
        )

    twelfth = 1.0 / 12.0

    def slopes(rows):
        def body(i, carry):
            at = pl.ds(pl.multiple_of(i * 8, 8), 8)
            y0 = i * 8 + PAD
            mid = {}
            for row in rows:
                for k in (-2, -1, 0, 1, 2):
                    if row + k not in mid:
                        mid[row + k] = log_buf[row + k, pl.ds(pl.multiple_of(y0, 8), 8), :]
            for row in rows:
                y = [log_buf[row, pl.ds(y0 + k, 8), :] for k in (-2, -1, 1, 2)]
                z = z_shifts(mid[row])
                x = [mid[row + k] for k in (-2, -1, 1, 2)]
                for axis, u in enumerate((x, y, z)):
                    grad[axis, row, at, :] = (8.0 * (u[2] - u[1]) - (u[3] - u[0])) * twelfth
                courant[row, at, :] = courant[row, at, :] * twelfth
            return carry

        lax.fori_loop(0, ny // 8, body, 0)

    cell = cell_ref[0]
    weight = weight_ref[0]

    def advance(dst, src, prev, rows, i, amplitude, snap=None):
        at = pl.ds(pl.multiple_of(i * 8, 8), 8)
        y0 = i * 8 + PAD
        centre = pl.ds(pl.multiple_of(y0, 8), 8)
        mid = {row: field[src, row, centre, :] for row in range(rows[0] - 2, rows[-1] + 3)}
        for row in rows:
            u = mid[row]
            y = [field[src, row, pl.ds(y0 + k, 8), :] for k in (-2, -1, 1, 2)]
            z = z_shifts(u)
            x = [mid[row + k] for k in (-2, -1, 1, 2)]
            near = (x[1] + x[2]) + (y[1] + y[2]) + (z[1] + z[2])
            far = (x[0] + x[3]) + (y[0] + y[3]) + (z[0] + z[3])
            drift = [
                grad[axis, row, at, :] * (8.0 * (v[2] - v[1]) - (v[3] - v[0]))
                for axis, v in enumerate((x, y, z))
            ]
            change = (16.0 * near - far - 90.0 * u) + (drift[0] + drift[1] + drift[2])
            new = (2.0 * u - field[prev, row, centre, :]) + courant[row, at, :] * change
            base = ((s * ROWS + (row - ROWS)) * ny + i * 8) * nz
            new = new + jnp.where(ids == cell - base, amplitude, 0.0)
            field[dst, row, centre, :] = new
            if snap is not None:
                weighted[snap, row - ROWS, at, :] = weight * new

    own_rows = range(ROWS, 2 * ROWS)
    wide_rows = range(ROWS - 2, 2 * ROWS + 2)
    per = chunk // 8

    def group_copy(k, other):
        d = lax.rem(other - member + group, group)
        return d, pltpu.make_async_remote_copy(
            src_ref=weighted.at[k, :, pl.ds(pl.multiple_of(other * block, 8), block)],
            dst_ref=group_in.at[k, jnp.maximum(d - 1, 0)],
            send_sem=group_send.at[k, jnp.maximum(d - 1, 0)],
            recv_sem=group_recv.at[k, jnp.maximum(d - 1, 0)],
            device_id=(s, rcv_of(other // CORES, zh, lax.rem(other, CORES))),
            device_id_type=MESH,
        )

    def group_start(k, j):
        for other in range(group // CHUNKS):
            d, copy = group_copy(k, j * (group // CHUNKS) + other)
            when(d > 0, copy.start)

    def group_wait(k, arrival):
        for d in range(1, group):
            copy = group_copy(k, lax.rem(member + d, group))[1]
            if arrival:
                copy.wait_recv()
            else:
                copy.wait_send()

    def tile_copies(out, landing, send, recv):
        for i in range(pairs):
            for c in range(CORES):
                z = core * pairs + i
                copy = pltpu.make_async_remote_copy(
                    src_ref=out.at[i, c],
                    dst_ref=landing.at[zh],
                    send_sem=send.at[i, c],
                    recv_sem=recv.at[zh],
                    device_id=(s, rcv_of(xpos, z, c)),
                    device_id_type=MESH,
                )
                yield i, c, (z == zh) & (c == core), copy

    def tile_arrive(landing, recv):
        for z in range(ZHI):
            copy = pltpu.make_async_remote_copy(
                src_ref=landing.at[z],
                dst_ref=landing.at[z],
                send_sem=recv.at[z],
                recv_sem=recv.at[z],
                device_id=(s, rcv_of(xpos, z, half)),
                device_id_type=MESH,
            )
            when((z != zh) | (half != core), copy.wait_recv)

    def tile_start(k):
        group_wait(k, True)
        out, landing = tile_out.at[k], tile_in.at[k]
        for i, c, self_target, copy in tile_copies(out, landing, tile_send.at[k], tile_recv.at[k]):
            at = (2 * i + c) * 4
            for row in range(ROWS):
                total = weighted[k, row, pl.ds(member * block + at, 4), :]
                for d in range(group - 1):
                    total = total + group_in[k, d, row, at : at + 4, :]
                out[i, c, row] = total

            @pl.when(self_target)
            def _():
                landing[zh] = out[i, c]

            when(jnp.logical_not(self_target), copy.start)

    def tile_sent(out, landing, send, recv):
        for i, c, self_target, copy in tile_copies(out, landing, send, recv):
            when(jnp.logical_not(self_target), copy.wait_send)

    def snap_tile_start():
        loads[4].wait()
        for d in range(1, group):
            snap_copy(d).wait_recv()
        for i, c, self_target, copy in tile_copies(snap_out, snap_tile, stile_send, stile_recv):
            at = (2 * i + c) * 4
            for k in range(SNAPS):
                slot = owner_ref[k]
                holder = (slot // (CORES * ZHI)) * CORES + lax.rem(slot, CORES)
                place = lax.rem(member - holder + 2 * group - 1, group)
                for row in range(ROWS):
                    snap_out[i, c, k, row] = snap_in[place, row, at : at + 4, :]

            @pl.when(self_target)
            def _():
                snap_tile[zh] = snap_out[i, c]

            when(jnp.logical_not(self_target), copy.start)

    loads[0].wait()
    loads[1].wait()
    for side in (0, 1):
        when(comes[side], model_copy(0, side).wait_recv)
    slopes(own_rows)
    loads[2].wait()
    loads[3].wait()

    def first(j, carry):
        halo_arrive(0, j, 2, A)

        def body(i, inner):
            advance(M, A, M, own_rows, i, trace_ref[0, 0])
            return inner

        lax.fori_loop(j * per, (j + 1) * per, body, 0)
        halo_start(1, j, 2, M)
        return carry

    lax.fori_loop(0, CHUNKS, first, 0)
    for which in (1, 2):
        for side in (0, 1):
            when(comes[side], model_copy(which, side).wait_recv)
    slopes((2, 3, 8, 9))

    def second(j, carry):
        halo_arrive(1, j, 2, M)

        def body(i, inner):
            advance(B, M, A, own_rows, i, trace_ref[0, 1], 0)
            return inner

        lax.fori_loop(j * per, (j + 1) * per, body, 0)
        halo_start(2, j, ROWS, B)
        group_start(0, j)
        return carry

    lax.fori_loop(0, CHUNKS, second, 0)
    snap_tile_start()
    halo_sent(0, 2, A, True)
    halo_sent(1, 2, M)

    def pair(p, carry):
        src = lax.rem(p, 2)
        dst = 1 - src

        @pl.when(p > 1)
        def _():
            halo_sent(p, ROWS, dst)

        def part(j, inner):
            @pl.when(j == 0)
            def _():
                halo_arrive(p + 1, 0, ROWS, src)

            @pl.when(j < CHUNKS - 1)
            def _():
                halo_arrive(p + 1, j + 1, ROWS, src)

            def middle(i, deep):
                advance(M, src, M, wide_rows, i, trace_ref[0, 2 * p])
                return deep

            lax.fori_loop(
                jnp.where(j == 0, 0, j * per + 1),
                jnp.minimum((j + 1) * per + 1, ny // 8),
                middle,
                0,
            )

            def final(i, deep):
                advance(dst, M, src, own_rows, i, trace_ref[0, 2 * p + 1], p)
                return deep

            lax.fori_loop(j * per, (j + 1) * per, final, 0)
            when(p < SNAPS - 1, lambda: halo_start(p + 2, j, ROWS, dst))
            group_start(p, j)

            @pl.when(p == SNAPS - 1)
            def _():
                at = pl.ds(pl.multiple_of(j * chunk, 8), chunk)
                there = pl.ds(pl.multiple_of(j * chunk + PAD, 8), chunk)
                pltpu.make_async_copy(
                    field.at[dst, own, there], after_ref.at[0, :, at], out_sem.at[j]
                ).start()

            return inner

        lax.fori_loop(0, CHUNKS, part, 0)
        tile_start(p - 1)
        return carry

    lax.fori_loop(1, SNAPS, pair, 0)
    tile_start(SNAPS - 1)

    halo_sent(SNAPS, ROWS, B)
    for which in range(3):
        for side in (0, 1):
            when(leaves[side], model_copy(which, side).wait_send)
    for d in range(1, group):
        snap_copy(d).wait_send()
    for k in range(SNAPS):
        group_wait(k, False)
        tile_sent(tile_out.at[k], tile_in.at[k], tile_send.at[k], tile_recv.at[k])
    tile_sent(snap_out, snap_tile, stile_send, stile_recv)
    for j in range(CHUNKS):
        at = pl.ds(j * chunk, chunk)
        there = pl.ds(j * chunk + PAD, chunk)
        pltpu.make_async_copy(field.at[A, own, there], after_ref.at[0, :, at], out_sem.at[j]).wait()

    tile_arrive(snap_tile, stile_recv)
    for k in range(SNAPS):
        tile_arrive(tile_in.at[k], tile_recv.at[k])
    result = jnp.zeros((ROWS, 4, nz), F32)
    for k in range(SNAPS):
        total = (tile_in[k, 0] + tile_in[k, 1]) + (tile_in[k, 2] + tile_in[k, 3])
        holder = lax.rem(owner_ref[k] // CORES, ZHI)
        result = result + total * snap_tile[holder, k]
    sens_ref[...] = result


def local(mesh, now, before, courant, log, store, owner, cells, traces, weights):
    rows, ny, nz = courant.shape
    slabs, receivers = mesh.shape["slab"], mesh.shape["rcv"]
    xs = receivers // (ZHI * CORES)
    group = xs * CORES
    block = ny // group
    pairs = ZHI // CORES
    any_space = pl.BlockSpec(memory_space=pl.ANY)
    scalar = pl.BlockSpec(memory_space=pltpu.SMEM)
    dma = pltpu.SemaphoreType.DMA
    tall = ny + 2 * PAD
    return pl.pallas_call(
        functools.partial(kernel, (slabs, xs, ny, nz)),
        out_shape=(
            jax.ShapeDtypeStruct((rows, ny // receivers, nz), F32),
            jax.ShapeDtypeStruct(now.shape, F32),
        ),
        in_specs=[any_space] * 5 + [scalar] * 4,
        out_specs=(pl.BlockSpec(memory_space=pltpu.VMEM), any_space),
        scratch_shapes=[
            pltpu.VMEM((3, 3 * ROWS, tall, nz), F32),
            pltpu.VMEM((3 * ROWS, tall, nz), F32),
            pltpu.VMEM((3 * ROWS, ny, nz), F32),
            pltpu.VMEM((3, 3 * ROWS, ny, nz), F32),
            pltpu.VMEM((SNAPS, ROWS, ny, nz), F32),
            pltpu.VMEM((SNAPS, group - 1, ROWS, block, nz), F32),
            pltpu.VMEM((SNAPS, pairs, CORES, ROWS, 4, nz), F32),
            pltpu.VMEM((SNAPS, ZHI, ROWS, 4, nz), F32),
            pltpu.VMEM((group, ROWS, block, nz), F32),
            pltpu.VMEM((pairs, CORES, SNAPS, ROWS, 4, nz), F32),
            pltpu.VMEM((ZHI, SNAPS, ROWS, 4, nz), F32),
            dma((5,)),
            dma((3, 2)),
            dma((3, 2)),
            dma((SNAPS + 1, 2, CHUNKS)),
            dma((SNAPS + 1, 2, CHUNKS)),
            dma((SNAPS, group - 1)),
            dma((SNAPS, group - 1)),
            dma((SNAPS, pairs, CORES)),
            dma((SNAPS, ZHI)),
            dma((group - 1,)),
            dma((group - 1,)),
            dma((pairs, CORES)),
            dma((ZHI,)),
            dma((CHUNKS,)),
        ],
        compiler_params=pltpu.CompilerParams(
            collective_id=0, has_side_effects=True, vmem_limit_bytes=40 * 1024 * 1024
        ),
        name="adjoint",
    )(now, before, courant, log, store, owner, cells, traces, weights)


def solution(mesh):
    placed = (
        P("rcv", "slab", None, None),
        P("rcv", "slab", None, None),
        P("slab", None, None),
        P("slab", None, None),
        P("rcv", "slab", None, None),
        P(),
        P("rcv"),
        P("rcv", None),
        P("rcv"),
    )
    return jax.shard_map(
        functools.partial(local, mesh),
        mesh=mesh,
        in_specs=placed,
        out_specs=(P("slab", "rcv", None), P("rcv", "slab", None, None)),
        check_vma=False,
    )
```

time: 784 us -> 80.5 us (0.10)
  the two profiles are of different devices: /device:TPU:1 before, /device:TPU:39 now
where the time goes in v1:
time: 80.5 us; the launch traced here: 80.2 us
  Pallas kernels  72.1 us (90%)
  local copies, waits for them, and re-layouts  6.05 us (8%)
  between operations  2 us (2%)
    pallas_call x1, Pallas kernels, local(): pl.pallas_call(functools.partial(kernel, (slabs, xs, ny, nz)), out_shape=...  72.1 us
    unnamed x16, local copies, waits for them, and re-layouts  6.05 us

profile of v1, /device:TPU:39, one launch (start us, length us, event | category | flops | bytes accessed | tf_op | source)
XLA Modules:
  0.0 80.2 jit_solution(6629039677422204927)
XLA Ops:
  1.3 0.0 copy-start.5
  1.3 0.0 copy-start.6
  2.0 0.0 copy-done.5
  2.0 0.0 copy-done.6
  2.0 0.0 copy-start
  2.0 0.9 %copy-done = f32[1,4,128,128]{3,2,1,0:T(8,128)S(1)} copy-done((f32[1,4,128,128]{3,2,1,0:T(8,128)S(1)}, f32[1,4,128,128]{3,2,1,0:T(8,128)}, u32[]{:S(2)}) %copy-start) | copy-done | bytes 262168
  2.9 0.0 copy-start.1
  2.9 0.9 %copy-done.1 = f32[1,4,128,128]{3,2,1,0:T(8,128)S(1)} copy-done((f32[1,4,128,128]{3,2,1,0:T(8,128)S(1)}, f32[1,4,128,128]{3,2,1,0:T(8,128)}, u32[]{:S(2)}) %copy-start.1) | copy-done | bytes 262168
  3.9 0.0 copy-start.2
  3.9 0.9 %copy-done.2 = f32[4,128,128]{2,1,0:T(8,128)S(1)} copy-done((f32[4,128,128]{2,1,0:T(8,128)S(1)}, f32[4,128,128]{2,1,0:T(8,128)}, u32[]{:S(2)}) %copy-start.2) | copy-done | bytes 262168
  4.8 0.0 copy-start.3
  4.8 0.9 %copy-done.3 = f32[4,128,128]{2,1,0:T(8,128)S(1)} copy-done((f32[4,128,128]{2,1,0:T(8,128)S(1)}, f32[4,128,128]{2,1,0:T(8,128)}, u32[]{:S(2)}) %copy-start.3) | copy-done | bytes 262168
  5.8 0.0 copy-start.4
  5.8 0.9 %copy-done.4 = f32[1,4,128,128]{3,2,1,0:T(8,128)S(1)} copy-done((f32[1,4,128,128]{3,2,1,0:T(8,128)S(1)}, f32[1,4,128,128]{3,2,1,0:T(8,128)}, u32[]{:S(2)}) %copy-start.4) | copy-done | bytes 262168
  6.7 72.1 %adjoint.1 = (f32[4,4,128]{2,1,0:T(4,128)S(1)}, f32[1,4,128,128]{3,2,1,0:T(8,128)S(1)}) custom-call(f32[1,4,128,128]{3,2,1,0:T(8,128)S(1)} %copy-done, f32[1,4,128,128]{3,2,1,0:T(8,128)S(1)} %copy-done.1, f32[4,128,128]{2,1,0:T(8,128)S(1)} %copy-done.2, f32[4,128,128]{2,1,0:T(8,128)S(1)} %copy-done.3, f32[1,4,128,128]{3,2,1,0:T(8,128)S(1)} %copy-done.4, ...), custom_call_target="tpu_custom_call" | custom-call | tf_op jit(solution)/shard_map/adjoint/pallas_call | solution.py:511
  78.9 0.6 copy.15
  79.5 0.7 copy.16
Async XLA Ops:
  1.3 0.7 copy-start.5
  1.3 0.7 copy-start.6
  2.0 1.0 %copy-start = (f32[1,4,128,128]{3,2,1,0:T(8,128)S(1)}, f32[1,4,128,128]{3,2,1,0:T(8,128)}, u32[]{:S(2)}) copy-start(f32[1,4,128,128]{3,2,1,0:T(8,128)} %now_ref.1) | copy-start | bytes 786436
  2.9 0.9 %copy-start.1 = (f32[1,4,128,128]{3,2,1,0:T(8,128)S(1)}, f32[1,4,128,128]{3,2,1,0:T(8,128)}, u32[]{:S(2)}) copy-start(f32[1,4,128,128]{3,2,1,0:T(8,128)} %before_ref.1) | copy-start | bytes 786436
  3.9 0.9 %copy-start.2 = (f32[4,128,128]{2,1,0:T(8,128)S(1)}, f32[4,128,128]{2,1,0:T(8,128)}, u32[]{:S(2)}) copy-start(f32[4,128,128]{2,1,0:T(8,128)} %courant_ref.1) | copy-start | bytes 786436
  4.8 0.9 %copy-start.3 = (f32[4,128,128]{2,1,0:T(8,128)S(1)}, f32[4,128,128]{2,1,0:T(8,128)}, u32[]{:S(2)}) copy-start(f32[4,128,128]{2,1,0:T(8,128)} %log_ref.1) | copy-start | bytes 786436
  5.8 0.9 %copy-start.4 = (f32[1,4,128,128]{3,2,1,0:T(8,128)S(1)}, f32[1,4,128,128]{3,2,1,0:T(8,128)}, u32[]{:S(2)}) copy-start(f32[1,4,128,128]{3,2,1,0:T(8,128)} %store_ref.1) | copy-start | bytes 786436

commit v2 on v1

--- a/solution.py
+++ b/solution.py
@@ -13,9 +13,11 @@
 STEPS = 8
 CORES = 2
 ZHI = 4
+ZLO = 4
 ROWS = 4
-CHUNKS = 4
+CHUNKS = 8
 PAD = 8
+PARCELS = ((0, 4), (4, 7), (7, 8))
 A, B, M = 0, 1, 2
 
 
@@ -42,11 +44,10 @@
     grad,
     weighted,
     group_in,
-    tile_out,
-    tile_in,
     snap_in,
-    snap_out,
+    parcel_out,
     snap_tile,
+    sum_tile,
     load_sem,
     model_send,
     model_recv,
@@ -54,13 +55,12 @@
     halo_recv,
     group_send,
     group_recv,
-    tile_send,
-    tile_recv,
     snap_send,
     snap_recv,
-    stile_send,
-    stile_recv,
+    parcel_send,
+    parcel_recv,
     out_sem,
+    relay,
 ):
     slabs, xs, ny, nz = dims
     group = xs * CORES
@@ -92,8 +92,25 @@
     for d in range(1, group):
         greet(s, peer(d))
     half = zh // pairs
-    for z in range(ZHI):
-        when((z != zh) | (half != core), lambda: greet(s, rcv_of(xpos, z, half)))
+
+    columns = slabs // ZLO
+    zline = zh * ZLO + s // columns
+    length = ZHI * ZLO
+
+    def along(d, c=core):
+        z = lax.rem(zline + d + length, length)
+        return lax.rem(z, ZLO) * columns + lax.rem(s, columns), rcv_of(xpos, z // ZLO, c)
+
+    for d in (-1, 1):
+        for c in range(CORES):
+            greet(*along(d, c))
+
+    def relay_signal(n):
+        for d in (-(2**n), 2**n):
+            pl.semaphore_signal(relay.at[n], 1, device_id=along(d), device_id_type=MESH)
+
+    def relay_wait(n):
+        pl.semaphore_wait(relay.at[n], 2)
 
     own = pl.ds(ROWS, ROWS)
     ycells = pl.ds(PAD, ny)
@@ -135,9 +152,8 @@
     when(jnp.logical_not(has_left), lambda: clear(0))
     when(jnp.logical_not(has_right), lambda: clear(2 * ROWS))
 
-    mine = (zh // pairs == core).astype(jnp.int32)
     neighbours = has_left.astype(jnp.int32) + has_right.astype(jnp.int32)
-    pl.semaphore_wait(barrier, neighbours + (group - 1) + ZHI - mine)
+    pl.semaphore_wait(barrier, neighbours + (group - 1) + 2 * CORES)
 
     def side_copy(side, src, dst, send, recv):
         return pltpu.make_async_remote_copy(
@@ -157,12 +173,33 @@
         far = (0, 2)[side]
         land_near = (2, 8)[side]
         land_far = (0, 10)[side]
+        part = pl.ds(pl.multiple_of(core * (ny // 2), 8), ny // 2)
+        shifted = pl.ds(pl.multiple_of(core * (ny // 2) + PAD, 8), ny // 2)
         if which == 2:
-            src, dst = courant_ref.at[near : near + 2], courant.at[land_near : land_near + 2]
+            src, dst = courant_ref.at[near : near + 2, part], courant.at[land_near : land_near + 2, part]
+        elif which == 1:
+            src, dst = log_ref.at[far : far + 2, part], log_buf.at[land_far : land_far + 2, shifted]
         else:
-            at, to = ((near, land_near), (far, land_far))[which]
-            src, dst = log_ref.at[at : at + 2], log_buf.at[to : to + 2, ycells]
+            src, dst = log_ref.at[near : near + 2], log_buf.at[land_near : land_near + 2, ycells]
         return side_copy(side, src, dst, model_send.at[which, side], model_recv.at[which, side])
+
+    def share_copy(which, side):
+        part = pl.ds(pl.multiple_of(core * (ny // 2), 8), ny // 2)
+        shifted = pl.ds(pl.multiple_of(core * (ny // 2) + PAD, 8), ny // 2)
+        if which == 2:
+            at = (2, 8)[side]
+            block_ref = courant.at[at : at + 2, part]
+        else:
+            at = (0, 10)[side]
+            block_ref = log_buf.at[at : at + 2, shifted]
+        return pltpu.make_async_remote_copy(
+            src_ref=block_ref,
+            dst_ref=block_ref,
+            send_sem=model_send.at[which + 2, side],
+            recv_sem=model_recv.at[which + 2, side],
+            device_id=(s, rcv_of(xpos, zh, 1 - core)),
+            device_id_type=MESH,
+        )
 
     def halo_copy(e, side, j, deep, slot, from_input=False):
         if deep == ROWS:
@@ -201,9 +238,7 @@
         when(leaves[side], model_copy(0, side).start)
     for j in range(CHUNKS):
         halo_start(0, j, 2, A, True)
-    for which in (1, 2):
-        for side in (0, 1):
-            when(leaves[side], model_copy(which, side).start)
+    relay_signal(0)
 
     def snap_copy(d):
         other = lax.rem(member + d, group)
@@ -244,13 +279,19 @@
                 for k in (-2, -1, 0, 1, 2):
                     if row + k not in mid:
                         mid[row + k] = log_buf[row + k, pl.ds(pl.multiple_of(y0, 8), 8), :]
+            results = []
             for row in rows:
                 y = [log_buf[row, pl.ds(y0 + k, 8), :] for k in (-2, -1, 1, 2)]
                 z = z_shifts(mid[row])
                 x = [mid[row + k] for k in (-2, -1, 1, 2)]
                 for axis, u in enumerate((x, y, z)):
-                    grad[axis, row, at, :] = (8.0 * (u[2] - u[1]) - (u[3] - u[0])) * twelfth
-                courant[row, at, :] = courant[row, at, :] * twelfth
+                    slope = (8.0 * (u[2] - u[1]) - (u[3] - u[0])) * twelfth
+                    results.append((axis, row, slope))
+            scaled = [(row, courant[row, at, :] * twelfth) for row in rows]
+            for axis, row, slope in results:
+                grad[axis, row, at, :] = slope
+            for row, value in scaled:
+                courant[row, at, :] = value
             return carry
 
         lax.fori_loop(0, ny // 8, body, 0)
@@ -258,33 +299,38 @@
     cell = cell_ref[0]
     weight = weight_ref[0]
 
-    def advance(dst, src, prev, rows, i, amplitude, snap=None):
-        at = pl.ds(pl.multiple_of(i * 8, 8), 8)
-        y0 = i * 8 + PAD
-        centre = pl.ds(pl.multiple_of(y0, 8), 8)
-        mid = {row: field[src, row, centre, :] for row in range(rows[0] - 2, rows[-1] + 3)}
-        for row in rows:
-            u = mid[row]
-            y = [field[src, row, pl.ds(y0 + k, 8), :] for k in (-2, -1, 1, 2)]
-            z = z_shifts(u)
-            x = [mid[row + k] for k in (-2, -1, 1, 2)]
-            near = (x[1] + x[2]) + (y[1] + y[2]) + (z[1] + z[2])
-            far = (x[0] + x[3]) + (y[0] + y[3]) + (z[0] + z[3])
-            drift = [
-                grad[axis, row, at, :] * (8.0 * (v[2] - v[1]) - (v[3] - v[0]))
-                for axis, v in enumerate((x, y, z))
-            ]
-            change = (16.0 * near - far - 90.0 * u) + (drift[0] + drift[1] + drift[2])
-            new = (2.0 * u - field[prev, row, centre, :]) + courant[row, at, :] * change
-            base = ((s * ROWS + (row - ROWS)) * ny + i * 8) * nz
-            new = new + jnp.where(ids == cell - base, amplitude, 0.0)
+    def advance(dst, src, prev, rows, start, amplitude, snap=None, blocks=2):
+        results = []
+        for offset in range(blocks):
+            i = start + offset
+            at = pl.ds(pl.multiple_of(i * 8, 8), 8)
+            y0 = i * 8 + PAD
+            centre = pl.ds(pl.multiple_of(y0, 8), 8)
+            mid = {row: field[src, row, centre, :] for row in range(rows[0] - 2, rows[-1] + 3)}
+            for row in rows:
+                u = mid[row]
+                y = [field[src, row, pl.ds(y0 + k, 8), :] for k in (-2, -1, 1, 2)]
+                z = z_shifts(u)
+                x = [mid[row + k] for k in (-2, -1, 1, 2)]
+                near = (x[1] + x[2]) + (y[1] + y[2]) + (z[1] + z[2])
+                far = (x[0] + x[3]) + (y[0] + y[3]) + (z[0] + z[3])
+                drift = [
+                    grad[axis, row, at, :] * (8.0 * (v[2] - v[1]) - (v[3] - v[0]))
+                    for axis, v in enumerate((x, y, z))
+                ]
+                change = (16.0 * near - far - 90.0 * u) + (drift[0] + drift[1] + drift[2])
+                new = (2.0 * u - field[prev, row, centre, :]) + courant[row, at, :] * change
+                base = ((s * ROWS + (row - ROWS)) * ny + i * 8) * nz
+                new = new + jnp.where(ids == cell - base, amplitude, 0.0)
+                results.append((row, at, centre, new))
+        for row, at, centre, new in results:
             field[dst, row, centre, :] = new
             if snap is not None:
                 weighted[snap, row - ROWS, at, :] = weight * new
 
     own_rows = range(ROWS, 2 * ROWS)
     wide_rows = range(ROWS - 2, 2 * ROWS + 2)
-    per = chunk // 8
+    per = chunk // 16
 
     def group_copy(k, other):
         d = lax.rem(other - member + group, group)
@@ -310,71 +356,80 @@
             else:
                 copy.wait_send()
 
-    def tile_copies(out, landing, send, recv):
-        for i in range(pairs):
-            for c in range(CORES):
-                z = core * pairs + i
-                copy = pltpu.make_async_remote_copy(
-                    src_ref=out.at[i, c],
-                    dst_ref=landing.at[zh],
-                    send_sem=send.at[i, c],
-                    recv_sem=recv.at[zh],
-                    device_id=(s, rcv_of(xpos, z, c)),
-                    device_id_type=MESH,
-                )
-                yield i, c, (z == zh) & (c == core), copy
-
-    def tile_arrive(landing, recv):
+    pieces = [(i, c, (2 * i + c) * 4) for i in range(pairs) for c in range(CORES)]
+
+    def landing(part, z):
+        lo, hi = PARCELS[part]
+        return snap_tile.at[z] if part == 0 else sum_tile.at[z, lo - SNAPS : hi - SNAPS]
+
+    def parcel_copy(part, i, c):
+        lo, hi = PARCELS[part]
+        z = core * pairs + i
+        return (z == zh) & (c == core), pltpu.make_async_remote_copy(
+            src_ref=parcel_out.at[i, c, lo:hi],
+            dst_ref=landing(part, zh),
+            send_sem=parcel_send.at[part, i, c],
+            recv_sem=parcel_recv.at[part, zh],
+            device_id=(s, rcv_of(xpos, z, c)),
+            device_id_type=MESH,
+        )
+
+    def parcel_start(part):
+        lo, hi = PARCELS[part]
+        for i, c, at in pieces:
+            to_self, copy = parcel_copy(part, i, c)
+            when(jnp.logical_not(to_self), copy.start)
+
+            @pl.when(to_self)
+            def _():
+                for n in range(lo, hi):
+                    landing(part, zh)[n - lo] = parcel_out[i, c, n]
+
+    def parcel_sent(part):
+        for i, c, at in pieces:
+            to_self, copy = parcel_copy(part, i, c)
+            when(jnp.logical_not(to_self), copy.wait_send)
+
+    def parcel_arrive(part):
         for z in range(ZHI):
             copy = pltpu.make_async_remote_copy(
-                src_ref=landing.at[z],
-                dst_ref=landing.at[z],
-                send_sem=recv.at[z],
-                recv_sem=recv.at[z],
+                src_ref=landing(part, z),
+                dst_ref=landing(part, z),
+                send_sem=parcel_recv.at[part, z],
+                recv_sem=parcel_recv.at[part, z],
                 device_id=(s, rcv_of(xpos, z, half)),
                 device_id_type=MESH,
             )
             when((z != zh) | (half != core), copy.wait_recv)
 
-    def tile_start(k):
+    def sum_tiles(k):
         group_wait(k, True)
-        out, landing = tile_out.at[k], tile_in.at[k]
-        for i, c, self_target, copy in tile_copies(out, landing, tile_send.at[k], tile_recv.at[k]):
-            at = (2 * i + c) * 4
+        results = []
+        for i, c, at in pieces:
             for row in range(ROWS):
-                total = weighted[k, row, pl.ds(member * block + at, 4), :]
-                for d in range(group - 1):
-                    total = total + group_in[k, d, row, at : at + 4, :]
-                out[i, c, row] = total
-
-            @pl.when(self_target)
-            def _():
-                landing[zh] = out[i, c]
-
-            when(jnp.logical_not(self_target), copy.start)
-
-    def tile_sent(out, landing, send, recv):
-        for i, c, self_target, copy in tile_copies(out, landing, send, recv):
-            when(jnp.logical_not(self_target), copy.wait_send)
-
-    def snap_tile_start():
+                terms = [weighted[k, row, pl.ds(member * block + at, 4), :]]
+                terms += [group_in[k, d, row, at : at + 4, :] for d in range(group - 1)]
+                while len(terms) > 1:
+                    terms = [a + b for a, b in zip(terms[::2], terms[1::2])]
+                results.append((i, c, row, terms[0]))
+        for i, c, row, total in results:
+            parcel_out[i, c, SNAPS + k, row] = total
+
+    def snap_tiles():
         loads[4].wait()
         for d in range(1, group):
             snap_copy(d).wait_recv()
-        for i, c, self_target, copy in tile_copies(snap_out, snap_tile, stile_send, stile_recv):
-            at = (2 * i + c) * 4
-            for k in range(SNAPS):
-                slot = owner_ref[k]
-                holder = (slot // (CORES * ZHI)) * CORES + lax.rem(slot, CORES)
-                place = lax.rem(member - holder + 2 * group - 1, group)
-                for row in range(ROWS):
-                    snap_out[i, c, k, row] = snap_in[place, row, at : at + 4, :]
-
-            @pl.when(self_target)
-            def _():
-                snap_tile[zh] = snap_out[i, c]
-
-            when(jnp.logical_not(self_target), copy.start)
+        for k in range(SNAPS):
+            slot = owner_ref[k]
+            holder = (slot // (CORES * ZHI)) * CORES + lax.rem(slot, CORES)
+            place = lax.rem(member - holder + 2 * group - 1, group)
+            results = [
+                (i, c, row, snap_in[place, row, at : at + 4, :])
+                for i, c, at in pieces
+                for row in range(ROWS)
+            ]
+            for i, c, row, value in results:
+                parcel_out[i, c, k, row] = value
 
     loads[0].wait()
     loads[1].wait()
@@ -383,12 +438,14 @@
     slopes(own_rows)
     loads[2].wait()
     loads[3].wait()
+    relay_wait(0)
+    relay_signal(1)
 
     def first(j, carry):
         halo_arrive(0, j, 2, A)
 
         def body(i, inner):
-            advance(M, A, M, own_rows, i, trace_ref[0, 0])
+            advance(M, A, M, own_rows, 2 * i, trace_ref[0, 0])
             return inner
 
         lax.fori_loop(j * per, (j + 1) * per, body, 0)
@@ -398,14 +455,15 @@
     lax.fori_loop(0, CHUNKS, first, 0)
     for which in (1, 2):
         for side in (0, 1):
-            when(comes[side], model_copy(which, side).wait_recv)
-    slopes((2, 3, 8, 9))
+            when(leaves[side], model_copy(which, side).start)
+    relay_wait(1)
+    relay_signal(2)
 
     def second(j, carry):
         halo_arrive(1, j, 2, M)
 
         def body(i, inner):
-            advance(B, M, A, own_rows, i, trace_ref[0, 1], 0)
+            advance(B, M, A, own_rows, 2 * i, trace_ref[0, 1], 0)
             return inner
 
         lax.fori_loop(j * per, (j + 1) * per, body, 0)
@@ -414,7 +472,17 @@
         return carry
 
     lax.fori_loop(0, CHUNKS, second, 0)
-    snap_tile_start()
+    for which in (1, 2):
+        for side in (0, 1):
+            when(comes[side], model_copy(which, side).wait_recv)
+            when(comes[side], share_copy(which, side).start)
+    snap_tiles()
+    relay_wait(2)
+    parcel_start(0)
+    for which in (1, 2):
+        for side in (0, 1):
+            when(comes[side], share_copy(which, side).wait)
+    slopes((2, 3, 8, 9))
     halo_sent(0, 2, A, True)
     halo_sent(1, 2, M)
 
@@ -435,24 +503,31 @@
             def _():
                 halo_arrive(p + 1, j + 1, ROWS, src)
 
-            def middle(i, deep):
-                advance(M, src, M, wide_rows, i, trace_ref[0, 2 * p])
+            def middle(start, blocks):
+                advance(M, src, M, wide_rows, start, trace_ref[0, 2 * p], None, blocks)
+
+            when(j == 0, lambda: middle(0, 1))
+
+            def ahead(i, deep):
+                when(i < ny // 16 - 1, lambda: middle(2 * i + 1, 2))
+                when(i == ny // 16 - 1, lambda: middle(2 * i + 1, 1))
                 return deep
 
-            lax.fori_loop(
-                jnp.where(j == 0, 0, j * per + 1),
-                jnp.minimum((j + 1) * per + 1, ny // 8),
-                middle,
-                0,
-            )
+            lax.fori_loop(j * per, (j + 1) * per, ahead, 0)
 
             def final(i, deep):
-                advance(dst, M, src, own_rows, i, trace_ref[0, 2 * p + 1], p)
+                advance(dst, M, src, own_rows, 2 * i, trace_ref[0, 2 * p + 1], p)
                 return deep
 
             lax.fori_loop(j * per, (j + 1) * per, final, 0)
             when(p < SNAPS - 1, lambda: halo_start(p + 2, j, ROWS, dst))
             group_start(p, j)
+
+            @pl.when((p == SNAPS - 1) & (j == CHUNKS - 2))
+            def _():
+                for k in range(SNAPS - 1):
+                    sum_tiles(k)
+                parcel_start(1)
 
             @pl.when(p == SNAPS - 1)
             def _():
@@ -465,11 +540,11 @@
             return inner
 
         lax.fori_loop(0, CHUNKS, part, 0)
-        tile_start(p - 1)
         return carry
 
     lax.fori_loop(1, SNAPS, pair, 0)
-    tile_start(SNAPS - 1)
+    sum_tiles(SNAPS - 1)
+    parcel_start(2)
 
     halo_sent(SNAPS, ROWS, B)
     for which in range(3):
@@ -479,22 +554,24 @@
         snap_copy(d).wait_send()
     for k in range(SNAPS):
         group_wait(k, False)
-        tile_sent(tile_out.at[k], tile_in.at[k], tile_send.at[k], tile_recv.at[k])
-    tile_sent(snap_out, snap_tile, stile_send, stile_recv)
     for j in range(CHUNKS):
         at = pl.ds(j * chunk, chunk)
         there = pl.ds(j * chunk + PAD, chunk)
         pltpu.make_async_copy(field.at[A, own, there], after_ref.at[0, :, at], out_sem.at[j]).wait()
 
-    tile_arrive(snap_tile, stile_recv)
-    for k in range(SNAPS):
-        tile_arrive(tile_in.at[k], tile_recv.at[k])
-    result = jnp.zeros((ROWS, 4, nz), F32)
-    for k in range(SNAPS):
-        total = (tile_in[k, 0] + tile_in[k, 1]) + (tile_in[k, 2] + tile_in[k, 3])
+    def kernel_term(k):
+        total = (sum_tile[0, k] + sum_tile[1, k]) + (sum_tile[2, k] + sum_tile[3, k])
         holder = lax.rem(owner_ref[k] // CORES, ZHI)
-        result = result + total * snap_tile[holder, k]
-    sens_ref[...] = result
+        return total * snap_tile[holder, k]
+
+    parcel_sent(0)
+    parcel_sent(1)
+    parcel_arrive(0)
+    parcel_arrive(1)
+    early = (kernel_term(0) + kernel_term(1)) + kernel_term(2)
+    parcel_arrive(2)
+    sens_ref[...] = early + kernel_term(SNAPS - 1)
+    parcel_sent(2)
 
 
 def local(mesh, now, before, courant, log, store, owner, cells, traces, weights):
@@ -504,7 +581,7 @@
     group = xs * CORES
     block = ny // group
     pairs = ZHI // CORES
-    any_space = pl.BlockSpec(memory_space=pl.ANY)
+    any_space = pl.BlockSpec(memory_space=pltpu.HBM)
     scalar = pl.BlockSpec(memory_space=pltpu.SMEM)
     dma = pltpu.SemaphoreType.DMA
     tall = ny + 2 * PAD
@@ -523,28 +600,26 @@
             pltpu.VMEM((3, 3 * ROWS, ny, nz), F32),
             pltpu.VMEM((SNAPS, ROWS, ny, nz), F32),
             pltpu.VMEM((SNAPS, group - 1, ROWS, block, nz), F32),
-            pltpu.VMEM((SNAPS, pairs, CORES, ROWS, 4, nz), F32),
-            pltpu.VMEM((SNAPS, ZHI, ROWS, 4, nz), F32),
             pltpu.VMEM((group, ROWS, block, nz), F32),
-            pltpu.VMEM((pairs, CORES, SNAPS, ROWS, 4, nz), F32),
+            pltpu.VMEM((pairs, CORES, 2 * SNAPS, ROWS, 4, nz), F32),
+            pltpu.VMEM((ZHI, SNAPS, ROWS, 4, nz), F32),
             pltpu.VMEM((ZHI, SNAPS, ROWS, 4, nz), F32),
             dma((5,)),
-            dma((3, 2)),
-            dma((3, 2)),
+            dma((5, 2)),
+            dma((5, 2)),
             dma((SNAPS + 1, 2, CHUNKS)),
             dma((SNAPS + 1, 2, CHUNKS)),
             dma((SNAPS, group - 1)),
             dma((SNAPS, group - 1)),
-            dma((SNAPS, pairs, CORES)),
-            dma((SNAPS, ZHI)),
             dma((group - 1,)),
             dma((group - 1,)),
-            dma((pairs, CORES)),
-            dma((ZHI,)),
+            dma((len(PARCELS), pairs, CORES)),
+            dma((len(PARCELS), ZHI)),
             dma((CHUNKS,)),
+            pltpu.SemaphoreType.REGULAR((3,)),
         ],
         compiler_params=pltpu.CompilerParams(
-            collective_id=0, has_side_effects=True, vmem_limit_bytes=40 * 1024 * 1024
+            collective_id=0, has_side_effects=True, vmem_limit_bytes=60 * 1024 * 1024
         ),
         name="adjoint",
     )(now, before, courant, log, store, owner, cells, traces, weights)

time: 80.5 us -> 71.9 us (0.89)
  the two profiles are of different devices: /device:TPU:39 before, /device:TPU:35 now
where the time goes in v2:
time: 71.9 us; the launch traced here: 71.7 us
  Pallas kernels  66.8 us (93%)
  local copies, waits for them, and re-layouts  2.97 us (4%)
  between operations  1.93 us (3%)
    pallas_call x1, Pallas kernels, local(): pl.pallas_call(functools.partial(kernel, (slabs, xs, ny, nz)), out_shape=...  66.8 us
    unnamed x2, local copies, waits for them, and re-layouts  2.97 us

profile of v2, /device:TPU:35, one launch (start us, length us, event | category | flops | bytes accessed | tf_op | source)
XLA Modules:
  0.0 71.7 jit_solution(4634975007724602983)
XLA Ops:
  1.9 66.8 %adjoint.1 = (f32[4,4,128]{2,1,0:T(4,128)}, f32[1,4,128,128]{3,2,1,0:T(8,128)}) custom-call(f32[1,4,128,128]{3,2,1,0:T(8,128)} %now_ref.1, f32[1,4,128,128]{3,2,1,0:T(8,128)} %before_ref.1, f32[4,128,128]{2,1,0:T(8,128)} %courant_ref.1, f32[4,128,128]{2,1,0:T(8,128)} %log_ref.1, f32[1,4,128,128]{3,2,1,0:T(8,128)} %store_ref.1, s32[32]{0:T(128)} %owner_ref.1, ...), custom_call_target="tpu_custom_call" | custom-call | tf_op jit(solution)/shard_map/adjoint/pallas_call | solution.py:588
  68.7 1.3 %copy.15 = f32[4,4,128]{2,1,0:T(4,128)} copy(f32[4,4,128]{2,1,0:T(4,128)} %get-tuple-element.4) | data formatting | bytes 16384
  70.0 1.7 %copy.16 = f32[1,4,128,128]{3,2,1,0:T(8,128)} copy(f32[1,4,128,128]{3,2,1,0:T(8,128)} %get-tuple-element.5) | data formatting | bytes 524288

commit v3 on v2

--- a/solution.py
+++ b/solution.py
@@ -177,10 +177,9 @@
         shifted = pl.ds(pl.multiple_of(core * (ny // 2) + PAD, 8), ny // 2)
         if which == 2:
             src, dst = courant_ref.at[near : near + 2, part], courant.at[land_near : land_near + 2, part]
-        elif which == 1:
-            src, dst = log_ref.at[far : far + 2, part], log_buf.at[land_far : land_far + 2, shifted]
         else:
-            src, dst = log_ref.at[near : near + 2], log_buf.at[land_near : land_near + 2, ycells]
+            at, to = ((near, land_near), (far, land_far))[which]
+            src, dst = log_ref.at[at : at + 2, part], log_buf.at[to : to + 2, shifted]
         return side_copy(side, src, dst, model_send.at[which, side], model_recv.at[which, side])
 
     def share_copy(which, side):
@@ -190,16 +189,25 @@
             at = (2, 8)[side]
             block_ref = courant.at[at : at + 2, part]
         else:
-            at = (0, 10)[side]
+            at = ((2, 8), (0, 10))[which][side]
             block_ref = log_buf.at[at : at + 2, shifted]
         return pltpu.make_async_remote_copy(
             src_ref=block_ref,
             dst_ref=block_ref,
-            send_sem=model_send.at[which + 2, side],
-            recv_sem=model_recv.at[which + 2, side],
+            send_sem=model_send.at[which + 3, side],
+            recv_sem=model_recv.at[which + 3, side],
             device_id=(s, rcv_of(xpos, zh, 1 - core)),
             device_id_type=MESH,
         )
+
+    def share_start(which):
+        for side in (0, 1):
+            when(comes[side], model_copy(which, side).wait_recv)
+            when(comes[side], share_copy(which, side).start)
+
+    def share_wait(which):
+        for side in (0, 1):
+            when(comes[side], share_copy(which, side).wait)
 
     def halo_copy(e, side, j, deep, slot, from_input=False):
         if deep == ROWS:
@@ -238,6 +246,9 @@
         when(leaves[side], model_copy(0, side).start)
     for j in range(CHUNKS):
         halo_start(0, j, 2, A, True)
+    for which in (1, 2):
+        for side in (0, 1):
+            when(leaves[side], model_copy(which, side).start)
     relay_signal(0)
 
     def snap_copy(d):
@@ -250,9 +261,6 @@
             device_id=(s, peer(d)),
             device_id_type=MESH,
         )
-
-    for d in range(1, group):
-        snap_copy(d).start()
 
     lane = lax.broadcasted_iota(jnp.int32, (8, nz), 1)
     ids = lax.broadcasted_iota(jnp.int32, (8, nz), 0) * nz + lane
@@ -433,9 +441,11 @@
 
     loads[0].wait()
     loads[1].wait()
-    for side in (0, 1):
-        when(comes[side], model_copy(0, side).wait_recv)
+    share_start(0)
+    share_wait(0)
     slopes(own_rows)
+    for d in range(1, group):
+        snap_copy(d).start()
     loads[2].wait()
     loads[3].wait()
     relay_wait(0)
@@ -454,8 +464,7 @@
 
     lax.fori_loop(0, CHUNKS, first, 0)
     for which in (1, 2):
-        for side in (0, 1):
-            when(leaves[side], model_copy(which, side).start)
+        share_start(which)
     relay_wait(1)
     relay_signal(2)
 
@@ -473,16 +482,11 @@
 
     lax.fori_loop(0, CHUNKS, second, 0)
     for which in (1, 2):
-        for side in (0, 1):
-            when(comes[side], model_copy(which, side).wait_recv)
-            when(comes[side], share_copy(which, side).start)
+        share_wait(which)
+    slopes((2, 3, 8, 9))
     snap_tiles()
     relay_wait(2)
     parcel_start(0)
-    for which in (1, 2):
-        for side in (0, 1):
-            when(comes[side], share_copy(which, side).wait)
-    slopes((2, 3, 8, 9))
     halo_sent(0, 2, A, True)
     halo_sent(1, 2, M)
 
@@ -495,6 +499,11 @@
             halo_sent(p, ROWS, dst)
 
         def part(j, inner):
+            @pl.when((p == SNAPS - 1) & (j == 0))
+            def _():
+                for k in range(SNAPS - 2):
+                    sum_tiles(k)
+
             @pl.when(j == 0)
             def _():
                 halo_arrive(p + 1, 0, ROWS, src)
@@ -525,8 +534,7 @@
 
             @pl.when((p == SNAPS - 1) & (j == CHUNKS - 2))
             def _():
-                for k in range(SNAPS - 1):
-                    sum_tiles(k)
+                sum_tiles(SNAPS - 2)
                 parcel_start(1)
 
             @pl.when(p == SNAPS - 1)
@@ -605,8 +613,8 @@
             pltpu.VMEM((ZHI, SNAPS, ROWS, 4, nz), F32),
             pltpu.VMEM((ZHI, SNAPS, ROWS, 4, nz), F32),
             dma((5,)),
-            dma((5, 2)),
-            dma((5, 2)),
+            dma((6, 2)),
+            dma((6, 2)),
             dma((SNAPS + 1, 2, CHUNKS)),
             dma((SNAPS + 1, 2, CHUNKS)),
             dma((SNAPS, group - 1)),

time: 71.9 us -> 71.3 us (level)
  the two profiles are of different devices: /device:TPU:35 before, /device:TPU:39 now
where the time goes in v3:
time: 71.3 us; the launch traced here: 71 us
  Pallas kernels  66.1 us (93%)
  local copies, waits for them, and re-layouts  2.97 us (4%)
  between operations  1.93 us (3%)
    pallas_call x1, Pallas kernels, local(): pl.pallas_call(functools.partial(kernel, (slabs, xs, ny, nz)), out_shape=...  66.1 us
    unnamed x2, local copies, waits for them, and re-layouts  2.97 us

profile of v3, /device:TPU:39, one launch (start us, length us, event | category | flops | bytes accessed | tf_op | source)
XLA Modules:
  0.0 71.0 jit_solution(17548281643634359867)
XLA Ops:
  1.9 66.1 %adjoint.1 = (f32[4,4,128]{2,1,0:T(4,128)}, f32[1,4,128,128]{3,2,1,0:T(8,128)}) custom-call(f32[1,4,128,128]{3,2,1,0:T(8,128)} %now_ref.1, f32[1,4,128,128]{3,2,1,0:T(8,128)} %before_ref.1, f32[4,128,128]{2,1,0:T(8,128)} %courant_ref.1, f32[4,128,128]{2,1,0:T(8,128)} %log_ref.1, f32[1,4,128,128]{3,2,1,0:T(8,128)} %store_ref.1, s32[32]{0:T(128)} %owner_ref.1, ...), custom_call_target="tpu_custom_call" | custom-call | tf_op jit(solution)/shard_map/adjoint/pallas_call | solution.py:596
  68.1 1.3 %copy.15 = f32[4,4,128]{2,1,0:T(4,128)} copy(f32[4,4,128]{2,1,0:T(4,128)} %get-tuple-element.4) | data formatting | bytes 16384
  69.4 1.7 %copy.16 = f32[1,4,128,128]{3,2,1,0:T(8,128)} copy(f32[1,4,128,128]{3,2,1,0:T(8,128)} %get-tuple-element.5) | data formatting | bytes 524288

commit v4 on v3

--- a/solution.py
+++ b/solution.py
@@ -444,8 +444,6 @@
     share_start(0)
     share_wait(0)
     slopes(own_rows)
-    for d in range(1, group):
-        snap_copy(d).start()
     loads[2].wait()
     loads[3].wait()
     relay_wait(0)
@@ -463,6 +461,8 @@
         return carry
 
     lax.fori_loop(0, CHUNKS, first, 0)
+    for d in range(1, group):
+        snap_copy(d).start()
     for which in (1, 2):
         share_start(which)
     relay_wait(1)
@@ -484,9 +484,7 @@
     for which in (1, 2):
         share_wait(which)
     slopes((2, 3, 8, 9))
-    snap_tiles()
     relay_wait(2)
-    parcel_start(0)
     halo_sent(0, 2, A, True)
     halo_sent(1, 2, M)
 
@@ -499,6 +497,11 @@
             halo_sent(p, ROWS, dst)
 
         def part(j, inner):
+            @pl.when((p == 1) & (j == CHUNKS - 2))
+            def _():
+                snap_tiles()
+                parcel_start(0)
+
             @pl.when((p == SNAPS - 1) & (j == 0))
             def _():
                 for k in range(SNAPS - 2):

time: 71.3 us -> 70.6 us (level)
  no operation moved by 1% of the time
where the time goes in v4:
time: 70.6 us; the launch traced here: 70.3 us
  Pallas kernels  65.4 us (93%)
  local copies, waits for them, and re-layouts  2.97 us (4%)
  between operations  1.93 us (3%)
    pallas_call x1, Pallas kernels, local(): pl.pallas_call(functools.partial(kernel, (slabs, xs, ny, nz)), out_shape=...  65.4 us
    unnamed x2, local copies, waits for them, and re-layouts  2.97 us

profile of v4, /device:TPU:39, one launch (start us, length us, event | category | flops | bytes accessed | tf_op | source)
XLA Modules:
  0.0 70.3 jit_solution(226379765555673810)
XLA Ops:
  1.9 65.4 %adjoint.1 = (f32[4,4,128]{2,1,0:T(4,128)}, f32[1,4,128,128]{3,2,1,0:T(8,128)}) custom-call(f32[1,4,128,128]{3,2,1,0:T(8,128)} %now_ref.1, f32[1,4,128,128]{3,2,1,0:T(8,128)} %before_ref.1, f32[4,128,128]{2,1,0:T(8,128)} %courant_ref.1, f32[4,128,128]{2,1,0:T(8,128)} %log_ref.1, f32[1,4,128,128]{3,2,1,0:T(8,128)} %store_ref.1, s32[32]{0:T(128)} %owner_ref.1, ...), custom_call_target="tpu_custom_call" | custom-call | tf_op jit(solution)/shard_map/adjoint/pallas_call | solution.py:599
  67.4 1.3 %copy.15 = f32[4,4,128]{2,1,0:T(4,128)} copy(f32[4,4,128]{2,1,0:T(4,128)} %get-tuple-element.4) | data formatting | bytes 16384
  68.7 1.7 %copy.16 = f32[1,4,128,128]{3,2,1,0:T(8,128)} copy(f32[1,4,128,128]{3,2,1,0:T(8,128)} %get-tuple-element.5) | data formatting | bytes 524288
